TPU v7x, 512 devices: a whole 4x4x16 slice. The times are simulated.
512 devices in a mesh: seq: 128 (over z, x, core), head: 4 (over y).
Axes of the slice: x: 4, y: 4, z: 16, core: 2. Of those that a mesh axis runs over, the one named last changes fastest.
Arguments:
- queries: bfloat16 [65536, 2048], P('seq', 'head'), may hold values from -6 to 6
- keys: bfloat16 [65536, 2048], P('seq', 'head'), may hold values from -6 to 6
- values: bfloat16 [65536, 2048], P('seq', 'head'), may hold values from -6 to 6
- grad_out: bfloat16 [65536, 2048], P('seq', 'head'), may hold values from -24 to 24
- out_weight: bfloat16 [2048, 2048], P('seq', 'head'), may hold values from -0.125 to 0.125
Outputs:
- query_grad: bfloat16 [65536, 2048], P('seq', 'head')
- key_grad: bfloat16 [65536, 2048], P('seq', 'head')
- value_grad: bfloat16 [65536, 2048], P('seq', 'head')
- weight_grad: float32 [2048, 2048], P('seq', 'head')
All inputs are finite; a program needn't handle non-finite values.
Results may differ from a plain program's by a relative error of at most 0.0057.
Values may be sent and summed in bfloat16 or wider, within the bound.
A program may use at most 192 MiB of HBM per device.

v0:
```python
import math
import jax
import jax.numpy as jnp
from jax import lax
from jax.sharding import PartitionSpec as P

HEAD_DIM = 128


def entering(x, axis, combine, identity, reverse):
    length, position = (lax.axis_size(axis), lax.axis_index(axis))
    everything = lax.all_gather(x, axis)
    start = jnp.broadcast_to(jnp.asarray(identity, x.dtype), x.shape)

    def hop(k, before):
        at = length - 1 - k if reverse else k
        reached = at > position if reverse else at < position
        new = combine(before, everything[at])
        return jnp.where(reached, new, before)

    return lax.fori_loop(0, length, hop, start)


def add_one(earlier, later):
    return earlier + later


def per_device(queries, keys, values, grad_out, out_weight):
    seq_count = lax.axis_size("seq")
    tok_rows, width = queries.shape
    heads = width // HEAD_DIM
    total_tokens = tok_rows * seq_count
    scale = 1.0 / math.sqrt(HEAD_DIM * total_tokens)
    grads_full = lax.all_gather(grad_out, "head", axis=1, tiled=True)
    weight_full = lax.all_gather(out_weight, "seq", axis=0, tiled=True)
    attn_grad = jnp.dot(grads_full, weight_full, preferred_element_type=jnp.float32).astype(
        jnp.bfloat16
    )
    q_heads = queries.reshape(tok_rows, heads, HEAD_DIM)
    k_heads = keys.reshape(tok_rows, heads, HEAD_DIM)
    v_heads = values.reshape(tok_rows, heads, HEAD_DIM)
    g_heads = attn_grad.reshape(tok_rows, heads, HEAD_DIM)
    kv_own = jnp.einsum("thi,thj->hij", k_heads, v_heads, preferred_element_type=jnp.float32)
    qg_own = jnp.einsum("thi,thj->hij", q_heads, g_heads, preferred_element_type=jnp.float32)
    zeros_state = jnp.zeros_like(kv_own)
    kv_prev = entering(kv_own, "seq", add_one, zeros_state, False)
    qg_next = entering(qg_own, "seq", add_one, zeros_state, True)
    prefix = kv_prev.astype(jnp.bfloat16)
    suffix = qg_next.astype(jnp.bfloat16)
    causal = jnp.tril(jnp.ones((tok_rows, tok_rows), bool))
    attn = jnp.where(
        causal[None],
        jnp.einsum("thi,shi->hts", q_heads, k_heads, preferred_element_type=jnp.float32),
        0.0,
    ).astype(jnp.bfloat16)
    back = jnp.where(
        causal[None],
        jnp.einsum("thj,shj->hts", g_heads, v_heads, preferred_element_type=jnp.float32),
        0.0,
    ).astype(jnp.bfloat16)
    out_rec = scale * (
        jnp.einsum("hts,shj->thj", attn, v_heads, preferred_element_type=jnp.float32)
        + jnp.einsum("thi,hij->thj", q_heads, prefix, preferred_element_type=jnp.float32)
    )
    out_flat = out_rec.astype(jnp.bfloat16).reshape(tok_rows, width)
    q_grad = scale * (
        jnp.einsum("hts,shi->thi", back, k_heads, preferred_element_type=jnp.float32)
        + jnp.einsum("thj,hij->thi", g_heads, prefix, preferred_element_type=jnp.float32)
    )
    k_grad = scale * (
        jnp.einsum("hts,thi->shi", back, q_heads, preferred_element_type=jnp.float32)
        + jnp.einsum("shj,hij->shi", v_heads, suffix, preferred_element_type=jnp.float32)
    )
    v_grad = scale * (
        jnp.einsum("hts,thj->shj", attn, g_heads, preferred_element_type=jnp.float32)
        + jnp.einsum("shi,hij->shj", k_heads, suffix, preferred_element_type=jnp.float32)
    )
    weight_grad = lax.psum_scatter(
        lax.dot_general(
            grads_full, out_flat, (((0,), (0,)), ((), ())), preferred_element_type=jnp.float32
        ),
        "seq",
        scatter_dimension=0,
        tiled=True,
    ) * (1.0 / math.sqrt(total_tokens))
    return (
        q_grad.astype(jnp.bfloat16).reshape(tok_rows, width),
        k_grad.astype(jnp.bfloat16).reshape(tok_rows, width),
        v_grad.astype(jnp.bfloat16).reshape(tok_rows, width),
        weight_grad,
    )


def solution(mesh):
    in_specs = (
        P("seq", "head"),
        P("seq", "head"),
        P("seq", "head"),
        P("seq", "head"),
        P("seq", "head"),
    )
    out_specs = (P("seq", "head"), P("seq", "head"), P("seq", "head"), P("seq", "head"))
    return jax.shard_map(
        per_device, mesh=mesh, in_specs=in_specs, out_specs=out_specs, check_vma=False
    )
```

profile of v0, /device:TPU:8, one launch (start us, length us, event | category | flops | bytes accessed | tf_op | source)
XLA Modules:
  0.0 860.1 jit_solution(12573711937423579405)
XLA Ops:
  8.7 1.3 copy.57
  10.0 2.1 fusion.15
  12.1 40.0 %all-gather.7.cloned.1.call-done = bf16[512,2048]{1,0:T(8,128)(2,1)} async-done(((bf16[512,512]{1,0:T(8,128)(2,1)}), bf16[512,2048]{1,0:T(8,128)(2,1)}) %all-gather.7.cloned.1.call-update) | async-done | bytes 2097168 | tf_op jit(solution)/shard_map/all_gather | solution.py:34
  52.1 144.0 %all-gather.9.cloned.1.call-done = bf16[2048,512]{1,0:T(8,128)(2,1)} async-done(((bf16[16,512]{1,0:T(8,128)(2,1)}), bf16[2048,512]{1,0:T(8,128)(2,1)}) %all-gather.9.cloned.1.call-update) | async-done | bytes 2097168 | tf_op jit(solution)/shard_map/all_gather | solution.py:35
  196.1 3.5 convolution_convert_fusion
  201.7 1.8 convolution_bitcast_fusion.2
  204.3 1.5 convolution_bitcast_fusion.1
  205.8 1.8 convolution_bitcast_fusion.3
  207.6 1.4 fusion.32
  209.1 182.3 %all-gather.11.cloned.1.call-done = f32[512,128,128]{2,1,0:T(8,128)} async-done(((f32[4,128,128]{2,1,0:T(8,128)}), f32[512,128,128]{2,1,0:T(8,128)}) %all-gather.11.cloned.1.call-update) | async-done | bytes 33554448 | tf_op jit(solution)/shard_map/all_gather | solution.py:12
  391.3 136.7 %while.30 = (s32[]{:T(128)}, f32[4,128,128]{2,1,0:T(8,128)S(1)}, s32[]{:T(128)}, f32[128,4,128,128]{3,2,1,0:T(8,128)}, s32[]{:T(128)}, /*index=5*/s32[]{:T(128)}) while((s32[]{:T(128)}, f32[4,128,128]{2,1,0:T(8,128)S(1)}, s32[]{:T(128)}, f32[128,4,128,128]{3,2,1,0:T(8,128)}, s32[]{:T(128)}, /*index=5*/s32[]{:T(128)}) %tuple.91), condition=%wide.region_1.2_spmd.clone, body=%wide.region_0.1_spmd.clone.sunk | while | flops 196612 | bytes 786533 | solution.py:21
  413.7 1.0 add_select_fusion.4
  479.7 1.1 add_select_fusion.4
  480.9 1.1 add_select_fusion.4
  482.0 1.1 add_select_fusion.4
  489.4 1.1 add_select_fusion.4
  494.8 1.1 add_select_fusion.4
  501.2 1.0 add_select_fusion.4
  506.6 1.1 add_select_fusion.4
  507.7 1.1 add_select_fusion.4
  516.2 1.1 add_select_fusion.4
  520.5 1.1 add_select_fusion.4
  524.8 1.1 add_select_fusion.4
  527.0 1.1 add_select_fusion.4
  528.1 1.6 fusion.7
  530.6 1.8 fusion.10
  532.6 3.3 convolution_bitcast_fusion
  535.9 5.5 copy.55
  541.4 45.1 %all-gather.13.cloned.1.call-done = f32[512,128,128]{2,1,0:T(8,128)} async-done(((f32[4,128,128]{2,1,0:T(8,128)}), f32[512,128,128]{2,1,0:T(8,128)}) %all-gather.13.cloned.1.call-update) | async-done | bytes 33554448 | tf_op jit(solution)/shard_map/all_gather | solution.py:12
  586.5 137.0 %while.31 = (s32[]{:T(128)}, f32[4,128,128]{2,1,0:T(8,128)S(1)}, s32[]{:T(128)}, f32[128,4,128,128]{3,2,1,0:T(8,128)}, s32[]{:T(128)}, /*index=5*/s32[]{:T(128)}, s32[]{:T(128)}, s32[]{:T(128)}) while((s32[]{:T(128)}, f32[4,128,128]{2,1,0:T(8,128)S(1)}, s32[]{:T(128)}, f32[128,4,128,128]{3,2,1,0:T(8,128)}, s32[]{:T(128)}, ...), condition=%wide.region_3.4_spmd.clone, body=%wide.region_2.3_spmd.clone.sunk | while | flops 196616 | bytes 786595 | solution.py:21
  723.6 1.6 fusion.8
  727.6 124.4 %reduce-scatter.4.cloned.1.call-done = f32[16,512]{1,0:T(8,128)} async-done(((f32[2048,512]{1,0:T(8,128)}), f32[16,512]{1,0:T(8,128)}) %reduce-scatter.4.cloned.1.call-update) | async-done | bytes 32784
  (275 shorter events, 262.8 us)
Async XLA Ops:
  7.2 192.5 %copy-start = (bf16[512,512]{1,0:T(8,128)(2,1)S(1)}, bf16[512,512]{1,0:T(8,128)(2,1)}, u32[]{:S(2)}) copy-start(bf16[512,512]{1,0:T(8,128)(2,1)} %param.9) | copy-start | bytes 1572868
  7.2 44.9 %all-gather.7.cloned.1.call-start = ((), (), s32[]{:S(2)}) async-start(), calls=%async_computation.1 | async-start | bytes 2621440 | tf_op jit(solution)/shard_map/all_gather | solution.py:34
  7.9 188.2 %all-gather.9.cloned.1.call-start = ((), (), s32[]{:S(2)}) async-start(), calls=%async_computation.2 | async-start | bytes 2113536 | tf_op jit(solution)/shard_map/all_gather | solution.py:35
  8.7 382.7 %all-gather.11.cloned.1.call-start = ((), (), s32[]{:S(2)}) async-start(), calls=%async_computation.3 | async-start | bytes 33816576 | tf_op jit(solution)/shard_map/all_gather | solution.py:12
  12.1 574.4 %all-gather.13.cloned.1.call-start = ((), (), s32[]{:S(2)}) async-start(), calls=%async_computation.4 | async-start | bytes 33816576 | tf_op jit(solution)/shard_map/all_gather | solution.py:12
  199.6 1.4 copy-start.1
  200.8 651.1 %reduce-scatter.4.cloned.1.call-start = ((), (), s32[]{:S(2)}) async-start(), calls=%async_computation.5 | async-start | bytes 4227072
  530.6 2.0 copy-start.3
  723.6 2.6 copy-start.2
Sparse Core Ops, SparseCore 0:
  10.1 41.9 all-gather.6
  55.2 140.7 all-gather.8
  199.8 191.4 all-gather.10
  394.9 191.5 all-gather.12
  591.0 260.8 reduce-scatter.3
where the time goes:
time: 868 us; the launch traced here: 860 us
  waiting for transfers between devices  537 us (62%)
  other arithmetic  267 us (31%)
  matrix products  22.5 us (3%)
  between operations  13.9 us (2%)
  local copies, waits for them, and re-layouts  12.4 us (1%)
    select_n x256, other arithmetic, hop(): return jnp.where(reached, new, before)  267 us
    all_gather x2, waiting for transfers between devices, entering(): everything = lax.all_gather(x, axis)  227 us
    all_gather x1, waiting for transfers between devices, per_device(): weight_full = lax.all_gather(out_weight, 'seq', axis=0, tiled=True)  144 us
    unnamed x6, waiting for transfers between devices  126 us
    all_gather x1, waiting for transfers between devices, per_device(): grads_full = lax.all_gather(grad_out, 'head', axis=1, tiled=True)  40 us
  transfers between devices with their start and end apart: 5, of which 5 were waited for; matrix products, arithmetic and copies ran while one was open for 35% of the time, Pallas kernels for 0%

commit v1 on v0

--- a/solution.py
+++ b/solution.py
@@ -31,7 +31,12 @@
     heads = width // HEAD_DIM
     total_tokens = tok_rows * seq_count
     scale = 1.0 / math.sqrt(HEAD_DIM * total_tokens)
-    grads_full = lax.all_gather(grad_out, "head", axis=1, tiled=True)
+    ring = [grad_out]
+    for hop_ in range(3):
+        ring.append(lax.ppermute(ring[-1], "head", [(dev, (dev + 1) % 4) for dev in range(4)]))
+    grads_full = jnp.roll(
+        jnp.concatenate(ring[::-1], axis=1), (lax.axis_index("head") + 1) * ring[0].shape[1], axis=1
+    )
     weight_full = lax.all_gather(out_weight, "seq", axis=0, tiled=True)
     attn_grad = jnp.dot(grads_full, weight_full, preferred_element_type=jnp.float32).astype(
         jnp.bfloat16

time: 868 us -> 828 us (0.954)
  waiting for transfers between devices: 537 us -> 482 us
  starting transfers between devices: 0.2 us -> 11.4 us
    unnamed x6 -> x4, waiting for transfers between devices: 126 us -> 0.73 us
    reduce_scatter x0 -> x1, waiting for transfers between devices: none -> 124 us  [per_device(): lax.psum_scatter(lax.dot_general(grads_full, out_flat, (((0,), (0,)), (()...]
    all_gather x1, waiting for transfers between devices: 144 us -> 93.5 us  [per_device(): weight_full = lax.all_gather(out_weight, 'seq', axis=0, tiled=True)]
    all_gather x1 -> x0, waiting for transfers between devices: 40 us -> none  [per_device(): grads_full = lax.all_gather(grad_out, 'head', axis=1, tiled=True)]
    ppermute x0 -> x3, waiting for transfers between devices: none -> 32.1 us  [per_device(): lax.ppermute(ring[-1], 'head', [(dev, (dev + 1) % 4) for dev in range(4)])]
    ppermute x0 -> x3, starting transfers between devices: none -> 11.2 us  [per_device(): lax.ppermute(ring[-1], 'head', [(dev, (dev + 1) % 4) for dev in range(4)])]
  transfers between devices with their start and end apart: 5 -> 7, of which waited for: 5 -> 7; matrix products, arithmetic and copies ran while one was open for 35% -> 37% of each run, Pallas kernels for 0% -> 0%
where the time goes in v1:
time: 828 us; the launch traced here: 819 us
  waiting for transfers between devices  482 us (58%)
  other arithmetic  269 us (32%)
  matrix products  23.9 us (3%)
  between operations  14 us (2%)
  local copies, waits for them, and re-layouts  12.3 us (1%)
  starting transfers between devices  11.4 us (1%)
    select_n x256, other arithmetic, hop(): return jnp.where(reached, new, before)  267 us
    all_gather x2, waiting for transfers between devices, entering(): everything = lax.all_gather(x, axis)  232 us
    reduce_scatter x1, waiting for transfers between devices, per_device(): lax.psum_scatter(lax.dot_general(grads_full, out_flat, (((0,), (0,)), (()...  124 us
    all_gather x1, waiting for transfers between devices, per_device(): weight_full = lax.all_gather(out_weight, 'seq', axis=0, tiled=True)  93.5 us
    ppermute x3, waiting for transfers between devices, per_device(): lax.ppermute(ring[-1], 'head', [(dev, (dev + 1) % 4) for dev in range(4)])  32.1 us
  transfers between devices with their start and end apart: 7, of which 7 were waited for; matrix products, arithmetic and copies ran while one was open for 37% of the time, Pallas kernels for 0%

profile of v1, /device:TPU:8, one launch (start us, length us, event | category | flops | bytes accessed | tf_op | source)
XLA Modules:
  0.0 819.2 jit_solution(18406866725549247743)
XLA Ops:
  8.0 1.3 copy.53
  9.2 2.1 fusion.22
  11.4 3.5 collective-permute-start
  14.9 12.3 %collective-permute-done = bf16[512,512]{1,0:T(8,128)(2,1)S(1)} collective-permute-done((bf16[512,512]{1,0:T(8,128)(2,1)}, bf16[512,512]{1,0:T(8,128)(2,1)S(1)}, u32[]{:S(2)}, u32[]{:S(2)}) %collective-permute-start) | collective-permute-done | bytes 524320 | tf_op jit(solution)/shard_map/ppermute | solution.py:36
  27.2 3.5 collective-permute-start.1
  30.6 10.4 %collective-permute-done.1 = bf16[512,512]{1,0:T(8,128)(2,1)S(1)} collective-permute-done((bf16[512,512]{1,0:T(8,128)(2,1)S(1)}, bf16[512,512]{1,0:T(8,128)(2,1)S(1)}, u32[]{:S(2)}, u32[]{:S(2)}) %collective-permute-start.1) | collective-permute-done | bytes 524320 | tf_op jit(solution)/shard_map/ppermute | solution.py:36
  41.0 4.3 collective-permute-start.2
  45.3 9.4 %collective-permute-done.2 = bf16[512,512]{1,0:T(8,128)(2,1)S(1)} collective-permute-done((bf16[512,512]{1,0:T(8,128)(2,1)S(1)}, bf16[512,512]{1,0:T(8,128)(2,1)S(1)}, u32[]{:S(2)}, u32[]{:S(2)}) %collective-permute-start.2) | collective-permute-done | bytes 524320 | tf_op jit(solution)/shard_map/ppermute | solution.py:36
  61.9 93.5 %all-gather.6.cloned.1.call-done = bf16[2048,512]{1,0:T(8,128)(2,1)} async-done(((bf16[16,512]{1,0:T(8,128)(2,1)}), bf16[2048,512]{1,0:T(8,128)(2,1)}) %all-gather.6.cloned.1.call-update) | async-done | bytes 2097168 | tf_op jit(solution)/shard_map/all_gather | solution.py:40
  155.4 3.5 fusion.15
  161.0 1.8 convolution_bitcast_fusion.1
  163.6 1.4 fusion.41
  165.0 1.5 convolution_bitcast_fusion
  166.5 1.8 convolution_bitcast_fusion.2
  168.3 182.3 %all-gather.8.cloned.1.call-done = f32[512,128,128]{2,1,0:T(8,128)} async-done(((f32[4,128,128]{2,1,0:T(8,128)}), f32[512,128,128]{2,1,0:T(8,128)}) %all-gather.8.cloned.1.call-update) | async-done | bytes 33554448 | tf_op jit(solution)/shard_map/all_gather | solution.py:12
  350.6 136.7 %while.30 = (s32[]{:T(128)}, f32[4,128,128]{2,1,0:T(8,128)S(1)}, s32[]{:T(128)}, f32[128,4,128,128]{3,2,1,0:T(8,128)}, s32[]{:T(128)}, /*index=5*/s32[]{:T(128)}) while((s32[]{:T(128)}, f32[4,128,128]{2,1,0:T(8,128)S(1)}, s32[]{:T(128)}, f32[128,4,128,128]{3,2,1,0:T(8,128)}, s32[]{:T(128)}, /*index=5*/s32[]{:T(128)}) %tuple.88), condition=%wide.region_1.2_spmd.clone, body=%wide.region_0.1_spmd.clone.sunk | while | flops 196612 | bytes 786533 | solution.py:21
  439.0 1.1 add_select_fusion.4
  440.1 1.1 add_select_fusion.4
  441.2 1.1 add_select_fusion.4
  448.7 1.1 add_select_fusion.4
  465.8 1.1 add_select_fusion.4
  467.0 1.1 add_select_fusion.4
  484.1 1.1 add_select_fusion.4
  486.2 1.1 add_select_fusion.4
  487.3 1.6 fusion.11
  489.9 1.6 fusion.14
  491.5 4.9 fusion
  496.4 49.5 %all-gather.10.cloned.1.call-done = f32[512,128,128]{2,1,0:T(8,128)} async-done(((f32[4,128,128]{2,1,0:T(8,128)}), f32[512,128,128]{2,1,0:T(8,128)}) %all-gather.10.cloned.1.call-update) | async-done | bytes 33554448 | tf_op jit(solution)/shard_map/all_gather | solution.py:12
  545.9 137.0 %while.31 = (s32[]{:T(128)}, f32[4,128,128]{2,1,0:T(8,128)S(1)}, s32[]{:T(128)}, f32[128,4,128,128]{3,2,1,0:T(8,128)}, s32[]{:T(128)}, /*index=5*/s32[]{:T(128)}, s32[]{:T(128)}, s32[]{:T(128)}) while((s32[]{:T(128)}, f32[4,128,128]{2,1,0:T(8,128)S(1)}, s32[]{:T(128)}, f32[128,4,128,128]{3,2,1,0:T(8,128)}, s32[]{:T(128)}, ...), condition=%wide.region_3.4_spmd.clone, body=%wide.region_2.3_spmd.clone.sunk | while | flops 196616 | bytes 786595 | solution.py:21
  683.0 1.6 fusion.13
  686.9 124.4 %reduce-scatter.2.cloned.1.call-done = f32[16,512]{1,0:T(8,128)} async-done(((f32[2048,512]{1,0:T(8,128)}), f32[16,512]{1,0:T(8,128)}) %reduce-scatter.2.cloned.1.call-update) | async-done | bytes 32784 | tf_op jit(solution)/shard_map/reduce_scatter | solution.py:83
  811.3 1.4 broadcast_multiply_fusion
  (283 shorter events, 272.5 us)
Async XLA Ops:
  7.2 151.7 %copy-start = (bf16[512,512]{1,0:T(8,128)(2,1)S(1)}, bf16[512,512]{1,0:T(8,128)(2,1)}, u32[]{:S(2)}) copy-start(bf16[512,512]{1,0:T(8,128)(2,1)} %param.9) | copy-start | bytes 1572868
  7.2 50.3 %copy-start.3 = (bf16[512,512]{1,0:T(8,128)(2,1)S(1)}, bf16[512,512]{1,0:T(8,128)(2,1)}, u32[]{:S(2)}) copy-start(bf16[512,512]{1,0:T(8,128)(2,1)} %param.12) | copy-start | bytes 1572868
  7.2 148.2 %all-gather.6.cloned.1.call-start = ((), (), s32[]{:S(2)}) async-start(), calls=%async_computation.1 | async-start | bytes 2113536 | tf_op jit(solution)/shard_map/all_gather | solution.py:40
  7.9 342.7 %all-gather.8.cloned.1.call-start = ((), (), s32[]{:S(2)}) async-start(), calls=%async_computation.3 | async-start | bytes 33816576 | tf_op jit(solution)/shard_map/all_gather | solution.py:12
  11.3 534.6 %all-gather.10.cloned.1.call-start = ((), (), s32[]{:S(2)}) async-start(), calls=%async_computation.4 | async-start | bytes 33816576 | tf_op jit(solution)/shard_map/all_gather | solution.py:12
  11.4 15.8 %collective-permute-start = (bf16[512,512]{1,0:T(8,128)(2,1)}, bf16[512,512]{1,0:T(8,128)(2,1)S(1)}, u32[]{:S(2)}, u32[]{:S(2)}) collective-permute-start(bf16[512,512]{1,0:T(8,128)(2,1)} %param.12), channel_id=1, source_target_pairs={{0,1},{1,2},{2,3},{3,0},{4,5},{5,6},{6,7},{7,4},{8,9},{9,10},{10,1... | collective-permute-start | bytes 1572872 | tf_op jit(solution)/shard_map/ppermute | solution.py:36
  27.2 13.9 %collective-permute-start.1 = (bf16[512,512]{1,0:T(8,128)(2,1)S(1)}, bf16[512,512]{1,0:T(8,128)(2,1)S(1)}, u32[]{:S(2)}, u32[]{:S(2)}) collective-permute-start(bf16[512,512]{1,0:T(8,128)(2,1)S(1)} %collective-permute-done), channel_id=1, source_target_pairs={{0,1},{1,2},{2,3},{3,0},{4,5},{5,6},{6,7},{7,4},{8,9},{9,10},{10,1... | collective-permute-start | bytes 1572872 | tf_op jit(solution)/shard_map/ppermute | solution.py:36
  41.0 13.7 %collective-permute-start.2 = (bf16[512,512]{1,0:T(8,128)(2,1)S(1)}, bf16[512,512]{1,0:T(8,128)(2,1)S(1)}, u32[]{:S(2)}, u32[]{:S(2)}) collective-permute-start(bf16[512,512]{1,0:T(8,128)(2,1)S(1)} %collective-permute-done.1), channel_id=1, source_target_pairs={{0,1},{1,2},{2,3},{3,0},{4,5},{5,6},{6,7},{7,4},{8,9},{9,10},{10,1... | collective-permute-start | bytes 1572872 | tf_op jit(solution)/shard_map/ppermute | solution.py:36
  61.9 98.3 %copy-start.1 = (bf16[512,512]{1,0:T(8,128)(2,1)S(1)}, bf16[512,512]{1,0:T(8,128)(2,1)}, u32[]{:S(2)}) copy-start(bf16[512,512]{1,0:T(8,128)(2,1)} %param.10) | copy-start | bytes 1572868
  160.0 651.2 %reduce-scatter.2.cloned.1.call-start = ((), (), s32[]{:S(2)}) async-start(), calls=%async_computation.2 | async-start | bytes 4227072 | tf_op jit(solution)/shard_map/reduce_scatter | solution.py:83
  496.4 189.1 %copy-start.2 = (f32[512,4,128]{0,2,1:T(8,128)S(1)}, f32[512,4,128]{0,2,1:T(8,128)}, u32[]{:S(2)}) copy-start(f32[512,4,128]{0,2,1:T(8,128)} %convolution_bitcast_fusion) | copy-start | bytes 3145732
Sparse Core Ops, SparseCore 0:
  11.2 144.1 all-gather.5
  159.1 191.4 all-gather.7
  354.3 191.5 all-gather.9
  550.5 260.7 reduce-scatter.1
